TPU v7x, 256 devices: a whole 4x4x8 slice. The times are simulated.
256 devices in a mesh: pass: 16 (over x, y), list: 16 (over z, core).
Axes of the slice: x: 4, y: 4, z: 8, core: 2. Of those that a mesh axis runs over, the one named last changes fastest.
Arguments:
- passages: bfloat16 [49152, 768], P('pass'), may hold values from -11 to 11
- centroids: bfloat16 [12288, 768], P('list'), may hold values from -0.21875 to 0.21875
Outputs:
- new_centroids: float32 [768, 12288], P('pass', 'list')
- list_potential: float32 [12288], P('list')
- passage_potential: float32 [49152], P('pass')
All inputs are finite; a program needn't handle non-finite values.
Results may differ from a plain program's by a relative error of at most 0.0023.
Values sent between devices are 32-bit elements; how exact they have to be, the bound alone decides.
A program may use at most 64 MiB of HBM per device.

v0:
```python
import math

import jax
import jax.numpy as jnp
from jax import lax
from jax.sharding import PartitionSpec as P

ITERS = 4


inv_temp = 20.0


def column_lse(shifted):
    local_max = jnp.max(shifted, axis=0)
    top = lax.pmax(local_max, "pass")
    total = lax.psum(jnp.sum(jnp.exp(shifted - top[None, :]), axis=0), "pass")
    return top + jnp.log(total)


def row_lse(moved):
    local_max = jnp.max(moved, axis=1)
    top = lax.pmax(local_max, "list")
    total = lax.psum(jnp.sum(jnp.exp(moved - top[:, None]), axis=1), "list")
    return top + jnp.log(total)


def local(passages, centroids):
    rows_here = passages.shape[0]
    lists_here = centroids.shape[0]
    logshare = math.log(rows_here * lax.axis_size("pass") / (lists_here * lax.axis_size("list")))
    kept_tile = (
        lax.dot_general(
            passages, centroids, (((1,), (1,)), ((), ())), preferred_element_type=jnp.float32
        )
        * inv_temp
    )
    row_pot = jnp.zeros((rows_here,), jnp.float32)
    col_pot = jnp.zeros((lists_here,), jnp.float32)
    for step in range(ITERS):
        tile = kept_tile
        col_pot = logshare - column_lse(tile + row_pot[:, None])
        row_pot = -row_lse(tile + col_pot[None, :])
    tile = kept_tile
    plan = jnp.exp(tile + row_pot[:, None] + col_pot[None, :])
    mass = lax.psum(jnp.sum(plan, axis=0), "pass")
    weights = plan.astype(jnp.bfloat16)
    term = lax.dot_general(
        passages, weights, (((0,), (0,)), ((), ())), preferred_element_type=jnp.float32
    )
    sums = lax.psum_scatter(term, "pass", scatter_dimension=0, tiled=True)
    new_centroids = sums / mass[None, :]
    return (new_centroids, col_pot, row_pot)


def solution(mesh):
    return jax.shard_map(
        local,
        mesh=mesh,
        in_specs=(P("pass", None), P("list", None)),
        out_specs=(P("pass", "list"), P("list"), P("pass")),
        check_vma=False,
    )
```

profile of v0, /device:TPU:32, one launch (start us, length us, event | category | flops | bytes accessed | tf_op | source)
XLA Modules:
  0.0 847.3 jit_solution(11747559081776375057)
XLA Ops:
  8.4 8.6 %fusion.9 = (f32[768]{0:T(1024)S(1)}, f32[3072,768]{1,0:T(8,128)}) fusion(bf16[3072,768]{1,0:T(8,128)(2,1)} %param.2, bf16[768,768]{1,0:T(8,128)(2,1)S(1)} %copy-done), kind=kOutput, calls=%fused_computation.32 | convolution fusion | flops 3628596480 | bytes 15338496 | tf_op jit(solution)/shard_map/dot_general | solution.py:33
  17.1 40.6 %pmax.56 = f32[768]{0:T(1024)S(1)} all-reduce(f32[768]{0:T(1024)S(1)} %get-tuple-element.9), channel_id=1, replica_groups=mesh['pass'=16,'list'=16] {'pass'}, use_global_device_ids=true, to_apply=%region_1.0 | all-reduce | flops 768 | bytes 6144 | tf_op jit(solution)/shard_map/pmax | solution.py:16
  57.7 5.0 exponential_reduce_fusion.7
  62.7 35.5 %psum.63 = f32[768]{0:T(1024)S(1)} all-reduce(f32[768]{0:T(1024)S(1)} %exponential_reduce_fusion.7), channel_id=1, replica_groups=mesh['pass'=16,'list'=16] {'pass'}, use_global_device_ids=true, to_apply=%region_3.0 | all-reduce | flops 768 | bytes 6144 | tf_op jit(solution)/shard_map/psum | solution.py:17
  102.6 45.3 %pmax.57 = f32[3072]{0:T(1024)S(1)} all-reduce(f32[3072]{0:T(1024)S(1)} %add_reduce_fusion.6), channel_id=1, replica_groups=mesh['pass'=16,'list'=16] {'list'}, use_global_device_ids=true, to_apply=%region_5.0 | all-reduce | flops 3072 | bytes 24576 | tf_op jit(solution)/shard_map/pmax | solution.py:23
  147.8 4.9 exponential_reduce_fusion.6
  152.7 45.7 %psum.64 = f32[3072]{0:T(1024)S(1)} all-reduce(f32[3072]{0:T(1024)S(1)} %exponential_reduce_fusion.6), channel_id=1, replica_groups=mesh['pass'=16,'list'=16] {'list'}, use_global_device_ids=true, to_apply=%region_7.0 | all-reduce | flops 3072 | bytes 24576 | tf_op jit(solution)/shard_map/psum | solution.py:24
  202.8 37.5 %pmax.58 = f32[768]{0:T(1024)S(1)} all-reduce(f32[768]{0:T(1024)S(1)} %add_reduce_fusion.5), channel_id=1, replica_groups=mesh['pass'=16,'list'=16] {'pass'}, use_global_device_ids=true, to_apply=%region_9.0 | all-reduce | flops 768 | bytes 6144 | tf_op jit(solution)/shard_map/pmax | solution.py:16
  245.0 35.5 %psum.65 = f32[768]{0:T(1024)S(1)} all-reduce(f32[768]{0:T(1024)S(1)} %exponential_reduce_fusion.5), channel_id=1, replica_groups=mesh['pass'=16,'list'=16] {'pass'}, use_global_device_ids=true, to_apply=%region_11.0 | all-reduce | flops 768 | bytes 6144 | tf_op jit(solution)/shard_map/psum | solution.py:17
  284.9 45.7 %pmax.59 = f32[3072]{0:T(1024)S(1)} all-reduce(f32[3072]{0:T(1024)S(1)} %add_reduce_fusion.4), channel_id=1, replica_groups=mesh['pass'=16,'list'=16] {'list'}, use_global_device_ids=true, to_apply=%region_13.0 | all-reduce | flops 3072 | bytes 24576 | tf_op jit(solution)/shard_map/pmax | solution.py:23
  330.6 4.9 exponential_reduce_fusion.4
  335.5 45.7 %psum.66 = f32[3072]{0:T(1024)S(1)} all-reduce(f32[3072]{0:T(1024)S(1)} %exponential_reduce_fusion.4), channel_id=1, replica_groups=mesh['pass'=16,'list'=16] {'list'}, use_global_device_ids=true, to_apply=%region_15.0 | all-reduce | flops 3072 | bytes 24576 | tf_op jit(solution)/shard_map/psum | solution.py:24
  385.6 37.6 %pmax.60 = f32[768]{0:T(1024)S(1)} all-reduce(f32[768]{0:T(1024)S(1)} %add_reduce_fusion.3), channel_id=1, replica_groups=mesh['pass'=16,'list'=16] {'pass'}, use_global_device_ids=true, to_apply=%region_17.0 | all-reduce | flops 768 | bytes 6144 | tf_op jit(solution)/shard_map/pmax | solution.py:16
  427.9 35.5 %psum.67 = f32[768]{0:T(1024)S(1)} all-reduce(f32[768]{0:T(1024)S(1)} %exponential_reduce_fusion.3), channel_id=1, replica_groups=mesh['pass'=16,'list'=16] {'pass'}, use_global_device_ids=true, to_apply=%region_19.0 | all-reduce | flops 768 | bytes 6144 | tf_op jit(solution)/shard_map/psum | solution.py:17
  467.8 45.7 %pmax.61 = f32[3072]{0:T(1024)S(1)} all-reduce(f32[3072]{0:T(1024)S(1)} %add_reduce_fusion.2), channel_id=1, replica_groups=mesh['pass'=16,'list'=16] {'list'}, use_global_device_ids=true, to_apply=%region_21.0 | all-reduce | flops 3072 | bytes 24576 | tf_op jit(solution)/shard_map/pmax | solution.py:23
  518.4 45.7 %psum.68 = f32[3072]{0:T(1024)S(1)} all-reduce(f32[3072]{0:T(1024)S(1)} %exponential_reduce_fusion.2), channel_id=1, replica_groups=mesh['pass'=16,'list'=16] {'list'}, use_global_device_ids=true, to_apply=%region_23.0 | all-reduce | flops 3072 | bytes 24576 | tf_op jit(solution)/shard_map/psum | solution.py:24
  568.5 37.5 %pmax.62 = f32[768]{0:T(1024)S(1)} all-reduce(f32[768]{0:T(1024)S(1)} %add_reduce_fusion.1), channel_id=1, replica_groups=mesh['pass'=16,'list'=16] {'pass'}, use_global_device_ids=true, to_apply=%region_25.0 | all-reduce | flops 768 | bytes 6144 | tf_op jit(solution)/shard_map/pmax | solution.py:16
  610.7 35.5 %psum.69 = f32[768]{0:T(1024)S(1)} all-reduce(f32[768]{0:T(1024)S(1)} %exponential_reduce_fusion.1), channel_id=1, replica_groups=mesh['pass'=16,'list'=16] {'pass'}, use_global_device_ids=true, to_apply=%region_27.0 | all-reduce | flops 768 | bytes 6144 | tf_op jit(solution)/shard_map/psum | solution.py:17
  650.5 45.7 %pmax.63 = f32[3072]{0:T(1024)S(1)} all-reduce(f32[3072]{0:T(1024)S(1)} %add_reduce_fusion), channel_id=1, replica_groups=mesh['pass'=16,'list'=16] {'list'}, use_global_device_ids=true, to_apply=%region_29.0 | all-reduce | flops 3072 | bytes 24576 | tf_op jit(solution)/shard_map/pmax | solution.py:23
  696.2 4.9 exponential_reduce_fusion
  701.2 45.9 %psum.70 = f32[3072]{0:T(1024)S(1)} all-reduce(f32[3072]{0:T(1024)S(1)} %exponential_reduce_fusion), channel_id=1, replica_groups=mesh['pass'=16,'list'=16] {'list'}, use_global_device_ids=true, to_apply=%region_31.0 | all-reduce | flops 3072 | bytes 24576 | tf_op jit(solution)/shard_map/psum | solution.py:24
  747.1 9.3 %fusion.6 = f32[768,768]{0,1:T(8,128)S(1)} fusion(bf16[3072,768]{1,0:T(8,128)(2,1)} %param.2, f32[3072,768]{1,0:T(8,128)} %get-tuple-element.10, f32[3072]{0:T(1024)S(1)} %add_negate_fusion, f32[768]{0:T(1024)S(1)} %add_subtract_fusion), kind=kOutput, calls=%fused_computation.22 | convolution fusion | flops 3630956544 | bytes 16530432 | tf_op jit(solution)/shard_map/dot_general | solution.py:48
  763.1 37.6 %psum.71 = f32[768]{0:T(1024)S(1)} all-reduce(f32[768]{0:T(1024)S(1)} %fusion), channel_id=1, replica_groups=mesh['pass'=16,'list'=16] {'pass'}, use_global_device_ids=true, to_apply=%region_34.0 | all-reduce | flops 768 | bytes 6144 | tf_op jit(solution)/shard_map/psum | solution.py:46
  800.7 37.7 %reduce-scatter.4.cloned.1.call-done = f32[48,768]{1,0:T(8,128)} async-done(((f32[768,768]{1,0:T(8,128)}), f32[48,768]{1,0:T(8,128)}) %reduce-scatter.4.cloned.1.call-update) | async-done | bytes 147472
  (32 shorter events, 59.7 us)
Async XLA Ops:
  7.2 1.3 copy-start
  7.2 831.2 %reduce-scatter.4.cloned.1.call-start = ((), (), s32[]{:S(2)}) async-start(), calls=%async_computation.1 | async-start | bytes 2506752
  646.2 112.2 %copy-start.1 = (f32[768]{0:T(1024)}, f32[768]{0:T(1024)S(1)}, u32[]{:S(2)}) copy-start(f32[768]{0:T(1024)S(1)} %add_subtract_fusion) | copy-start | bytes 9220
  747.1 11.3 %copy-start.2 = (f32[3072]{0:T(1024)}, f32[3072]{0:T(1024)S(1)}, u32[]{:S(2)}) copy-start(f32[3072]{0:T(1024)S(1)} %add_negate_fusion) | copy-start | bytes 36868
Sparse Core Ops, SparseCore 0:
  758.5 79.8 reduce-scatter.3
where the time goes:
time: 848 us; the launch traced here: 847 us
  blocking collectives  698 us (82%)
  other arithmetic  74.3 us (9%)
  waiting for transfers between devices  37.7 us (4%)
  matrix products  17.9 us (2%)
  between operations  14.2 us (2%)
    psum x4, blocking collectives, row_lse(): total = lax.psum(jnp.sum(jnp.exp(moved - top[:, None]), axis=1), 'list')  183 us
    pmax x4, blocking collectives, row_lse(): top = lax.pmax(local_max, 'list')  182 us
    pmax x4, blocking collectives, column_lse(): top = lax.pmax(local_max, 'pass')  153 us
    psum x4, blocking collectives, column_lse(): total = lax.psum(jnp.sum(jnp.exp(shifted - top[None, :]), axis=0), 'pass')  142 us
    unnamed x2, waiting for transfers between devices  37.7 us
    psum x1, blocking collectives, local(): mass = lax.psum(jnp.sum(plan, axis=0), 'pass')  37.6 us
    reduce_sum x4, other arithmetic, row_lse(): total = lax.psum(jnp.sum(jnp.exp(moved - top[:, None]), axis=1), 'list')  19.7 us
    reduce_sum x4, other arithmetic, column_lse(): total = lax.psum(jnp.sum(jnp.exp(shifted - top[None, :]), axis=0), 'pass')  19.1 us
  transfers between devices with their start and end apart: 1, of which 1 were waited for; matrix products, arithmetic and copies ran while one was open for 1% of the time, Pallas kernels for 0%

commit v1 on v0

v1 whole, which is shorter than its diff:
```python
import functools
import math

import jax
import jax.numpy as jnp
from jax import lax
from jax.experimental import pallas as pl
from jax.experimental.pallas import tpu as pltpu
from jax.sharding import PartitionSpec as P

ITERS = 4
INV_TEMP = 20.0
LOG2E = math.log2(math.e)
LN2 = math.log(2.0)
F32 = jnp.float32
BF16 = jnp.bfloat16
MESH = pl.DeviceIdType.MESH
CHUNK = 512
GROUP = 256
LINKS = (4, 12, 1, 3)
ORDERS = ((0, 1, 2, 3), (1, 0, 3, 2), (2, 3, 0, 1), (3, 2, 1, 0))


def flip(index, bits):
    out = index
    b = 1
    while b <= bits:
        if bits & b:
            out = out + b * (1 - 2 * ((index // b) % 2))
        b *= 2
    return out


def place_of(order):
    first = order[0]
    axis_bits = lambda seq, unit: [0, unit * seq[1], unit * seq[0], unit * (seq[0] ^ seq[1])]
    low = {0: 1, 1: 3, 2: 1, 3: 3}
    unit = {0: 4, 1: 4, 2: 1, 3: 1}
    major = axis_bits((low[order[0]], low[order[1]]), unit[first])
    minor = axis_bits((low[order[2]], low[order[3]]), unit[order[2]])
    return [a + b for a in major for b in minor]


PLACES = [place_of(order) for order in ORDERS]


def tree(values, op):
    while len(values) > 1:
        values = [op(values[i], values[i + 1]) for i in range(0, len(values), 2)]
    return values[0]


def lse2(values):
    top = tree(values, jnp.maximum)
    total = tree([jnp.exp2(v - top) for v in values], lax.add)
    return top + jnp.log(total) * LOG2E


def kernel(
    share,
    pas_hbm, cen_hbm,
    out_ref, cp_ref, rp_ref,
    cen, pas, tile, pas_t, wts, stag, rb0, rb1, rb2, rb3,
    lane_a, lane_b, csrc, cslot, rsrc, rpair, rmid, rslot, u_ref, w_ref, m_ref,
    in_sem, cs, cr, ps, pr, zs, zr, ss, sr,
):
    rows, depth = pas.shape
    lists = cen.shape[0]
    nrow, ncol = rows // 128, lists // 128
    p, l = lax.axis_index("pass"), lax.axis_index("list")
    rbs = (rb0, rb1, rb2, rb3)

    loads = [pltpu.make_async_copy(cen_hbm, cen, in_sem.at[0])]
    for b in range(rows // CHUNK):
        part = pl.ds(b * CHUNK, CHUNK)
        loads.append(pltpu.make_async_copy(pas_hbm.at[part], pas.at[part], in_sem.at[b + 1]))
    for load in loads:
        load.start()

    barrier = pltpu.get_barrier_semaphore()
    for k in range(1, 16):
        pl.semaphore_signal(barrier, inc=1, device_id=(flip(p, k), l), device_id_type=MESH)
    for k in (1, 2, 4, 6, 8, 10, 12, 14):
        pl.semaphore_signal(barrier, inc=1, device_id=(p, flip(l, k)), device_id_type=MESH)

    def col_send(i):
        for k in range(1, 16):
            pltpu.make_async_remote_copy(
                src_ref=csrc.at[i], dst_ref=cslot.at[i, k - 1], send_sem=cs, recv_sem=cr.at[i],
                device_id=(flip(p, k), l), device_id_type=MESH,
            ).start()

    def col_recv(i):
        pltpu.make_async_copy(cslot.at[i], cslot.at[i], cr.at[i]).wait()
        return [csrc[i]] + [cslot[i, k] for k in range(15)]

    def row_exchange(i, combine):
        copy = pltpu.make_async_remote_copy(
            src_ref=rsrc.at[i], dst_ref=rpair.at[i], send_sem=ps, recv_sem=pr.at[i],
            device_id=(p, flip(l, 1)), device_id_type=MESH,
        )
        copy.start()
        copy.wait_recv()
        rmid[i] = combine([rsrc[i], rpair[i]])
        for k in range(1, 8):
            pltpu.make_async_remote_copy(
                src_ref=rmid.at[i], dst_ref=rslot.at[i, k - 1], send_sem=zs, recv_sem=zr.at[i],
                device_id=(p, flip(l, 2 * k)), device_id_type=MESH,
            ).start()
        pltpu.make_async_copy(rslot.at[i], rslot.at[i], zr.at[i]).wait()
        return combine([rmid[i]] + [rslot[i, k] for k in range(7)])

    def spread(values):
        for k in range(ncol):
            lane_b[k * 128:(k + 1) * 128, :] = jnp.broadcast_to(values[k:k + 1, :], (128, 128)).T

    def fold(i):
        for k in range(ncol):
            csrc[i, k:k + 1, :] = jnp.sum(lane_a[k * 128:(k + 1) * 128, :].T, axis=0, keepdims=True)

    loads[0].wait()
    for b in range(rows // CHUNK):
        loads[b + 1].wait()
        tile[:, b * CHUNK:(b + 1) * CHUNK] = lax.dot_general(
            cen[...], pas[b * CHUNK:(b + 1) * CHUNK, :], (((1,), (1,)), ((), ())),
            preferred_element_type=F32,
        ) * (INV_TEMP * LOG2E)

    def col_first(r, carry):
        base = pl.ds(pl.multiple_of(r * 8, 8), 8)
        parts = [tile[base, c * 128:(c + 1) * 128] for c in range(nrow)]
        top = functools.reduce(jnp.maximum, parts)
        lane_a[base, :] = top
        lane_b[base, :] = functools.reduce(lax.add, [jnp.exp2(part - top) for part in parts])
        return carry

    lax.fori_loop(0, lists // 8, col_first, 0, unroll=2)
    for k in range(ncol):
        tops = lane_a[k * 128:(k + 1) * 128, :].T
        sums = lane_b[k * 128:(k + 1) * 128, :].T
        top = jnp.max(tops, axis=0, keepdims=True)
        total = jnp.sum(sums * jnp.exp2(tops - top), axis=0, keepdims=True)
        csrc[0, k:k + 1, :] = top + jnp.log(total) * LOG2E
    pl.semaphore_wait(barrier, 23)
    col_send(0)
    for b in range(rows // CHUNK):
        turned = pas[b * CHUNK:(b + 1) * CHUNK, :].T
        pas_t[:, :, b * CHUNK:(b + 1) * CHUNK] = turned.reshape(16, depth // 16, CHUNK)
    col_pot = share * LOG2E - lse2(col_recv(0))
    spread(col_pot)

    for b in range(rows // CHUNK):
        cols = [slice(b * CHUNK + c * 128, b * CHUNK + (c + 1) * 128) for c in range(CHUNK // 128)]

        def row_top(r, tops, cols=cols):
            base = pl.ds(pl.multiple_of(r * 8, 8), 8)
            add = lane_b[base, :]
            return tuple(jnp.maximum(top, tile[base, col] + add) for top, col in zip(tops, cols))

        tops = lax.fori_loop(
            0, lists // 8, row_top, tuple(jnp.full((8, 128), -jnp.inf, F32) for _ in cols), unroll=8
        )
        tops = [jnp.max(top, axis=0, keepdims=True) for top in tops]
        wide = [jnp.broadcast_to(top, (8, 128)) for top in tops]

        def row_exp(r, sums, cols=cols, wide=wide):
            base = pl.ds(pl.multiple_of(r * 8, 8), 8)
            add = lane_b[base, :]
            out = []
            for total, col, top in zip(sums, cols, wide):
                e = jnp.exp2(tile[base, col] + add - top)
                tile[base, col] = e
                out.append(total + e)
            return tuple(out)

        sums = lax.fori_loop(
            0, lists // 8, row_exp, tuple(jnp.zeros((8, 128), F32) for _ in cols), unroll=8
        )
        for c, (top, total) in enumerate(zip(tops, sums)):
            at = b * (CHUNK // 128) + c
            total = jnp.sum(total, axis=0, keepdims=True)
            m_ref[at:at + 1, :] = top
            rsrc[0, at:at + 1, :] = top + jnp.log(total) * LOG2E
    row_pot = -row_exchange(0, lse2)
    w_ref[...] = jnp.exp2(m_ref[...] + row_pot)
    u_ref[...] = w_ref[...]
    rp_ref[...] = row_pot * LN2
    cp_ref[...] = col_pot * LN2

    col_fac = row_fac = None
    for step in range(1, ITERS):
        us = [jnp.broadcast_to(u_ref[c:c + 1, :], (8, 128)) for c in range(nrow)]

        def col_sum(r, carry, us=us):
            base = pl.ds(pl.multiple_of(r * 8, 8), 8)
            lane_a[base, :] = tree_sum([tile[base, c * 128:(c + 1) * 128] * us[c] for c in range(nrow)])
            return carry

        lax.fori_loop(0, lists // 8, col_sum, 0, unroll=4)
        fold(step)
        col_send(step)
        col_fac = math.exp(share) / tree(col_recv(step), lax.add)
        spread(col_fac)
        for b in range(rows // CHUNK):
            cols = [slice(b * CHUNK + c * 128, b * CHUNK + (c + 1) * 128) for c in range(CHUNK // 128)]

            def row_sum(r, sums, cols=cols):
                base = pl.ds(pl.multiple_of(r * 8, 8), 8)
                fac = lane_b[base, :]
                return tuple(total + tile[base, col] * fac for total, col in zip(sums, cols))

            sums = lax.fori_loop(
                0, lists // 8, row_sum, tuple(jnp.zeros((8, 128), F32) for _ in cols), unroll=8
            )
            for c, total in enumerate(sums):
                at = b * (CHUNK // 128) + c
                rsrc[step, at:at + 1, :] = (
                    jnp.sum(total, axis=0, keepdims=True) * w_ref[at:at + 1, :]
                )
        row_fac = 1.0 / row_exchange(step, lambda values: tree(values, lax.add))
        u_ref[...] = w_ref[...] * row_fac
    rp_ref[...] += jnp.log(row_fac)
    cp_ref[...] += jnp.log(col_fac)

    us = [jnp.broadcast_to(u_ref[c:c + 1, :], (8, 128)) for c in range(nrow)]

    def plan(r, carry):
        base = pl.multiple_of(r * 16, 16)
        low, high = pl.ds(base, 8), pl.ds(base + 8, 8)
        first, second = [], []
        fac_low, fac_high = lane_b[low, :], lane_b[high, :]
        for c in range(nrow):
            col = slice(c * 128, (c + 1) * 128)
            a, b = tile[low, col] * us[c] * fac_low, tile[high, col] * us[c] * fac_high
            first.append(a)
            second.append(b)
            wts[pl.ds(base, 16), col] = jnp.concatenate([a, b], axis=0).astype(BF16)
        lane_a[low, :] = tree_sum(first)
        lane_a[high, :] = tree_sum(second)
        return carry

    lax.fori_loop(0, lists // 16, plan, 0)
    fold(ITERS)
    col_send(ITERS)

    half = depth // 32
    groups = lists // GROUP

    def hop(g, v, s):
        n = 8 >> s
        return pltpu.make_async_remote_copy(
            src_ref=stag.at[g, v, pl.ds(n, n)], dst_ref=rbs[s].at[g, v], send_sem=ss.at[s],
            recv_sem=sr.at[g, v, s], device_id=(flip(p, LINKS[ORDERS[v][s]]), l), device_id_type=MESH,
        )

    for g in range(groups):
        w = wts[g * GROUP:(g + 1) * GROUP, :]
        for q in range(4):
            left = jnp.concatenate([pas_t[flip(p, 4 * q + i)] for i in range(4)], axis=0)
            res = lax.dot_general(left, w, (((1,), (1,)), ((), ())), preferred_element_type=F32)
            for v in range(4):
                h, c = v // 2, v % 2
                for i in range(4):
                    stag[g, v, PLACES[v].index(4 * q + i)] = res[
                        i * 2 * half + h * half:i * 2 * half + (h + 1) * half, c * 128:(c + 1) * 128]
        for v in range(4):
            hop(g, v, 0).start()
    mass = None
    for s in range(1, 5):
        for g in range(groups):
            for v in range(4):
                hop(g, v, s - 1).wait_recv()
                n = 16 >> s
                if s < 4:
                    for i in list(range(n // 2, n)):
                        stag[g, v, i] += rbs[s - 1][g, v, i]
                    hop(g, v, s).start()
                    for i in range(n // 2):
                        stag[g, v, i] += rbs[s - 1][g, v, i]
                else:
                    if mass is None:
                        mass = tree(col_recv(ITERS), lax.add)
                    h, c = v // 2, v % 2
                    at = g * (GROUP // 128) + c
                    out_ref[h * half:(h + 1) * half, at * 128:(at + 1) * 128] = (
                        stag[g, v, 0] + rb3[g, v, 0]) / mass[at:at + 1, :]

    pltpu.make_async_copy(cslot, cslot, cs).wait()
    pltpu.make_async_copy(rpair, rpair, ps).wait()
    pltpu.make_async_copy(rslot, rslot, zs).wait()
    for s in range(4):
        pltpu.make_async_copy(rbs[s], rbs[s], ss.at[s]).wait()


def tree_sum(values):
    values = list(values)
    while len(values) > 1:
        pairs = [values[i] + values[i + 1] for i in range(0, len(values) - 1, 2)]
        values = pairs + values[len(values) - len(values) % 2:]
    return values[0]


def local(n_pass, n_list, passages, centroids):
    rows, depth = passages.shape
    lists = centroids.shape[0]
    nrow, ncol = rows // 128, lists // 128
    share = math.log(rows * n_pass / (lists * n_list))
    groups, part = lists // GROUP, depth // 32
    dma = pltpu.SemaphoreType.DMA
    vmem = pltpu.VMEM
    out, cp, rp = pl.pallas_call(
        functools.partial(kernel, share),
        out_shape=(
            jax.ShapeDtypeStruct((depth // n_pass, lists), F32),
            jax.ShapeDtypeStruct((ncol, 128), F32),
            jax.ShapeDtypeStruct((nrow, 128), F32),
        ),
        in_specs=[pl.BlockSpec(memory_space=pl.ANY)] * 2,
        out_specs=[pl.BlockSpec(memory_space=pltpu.VMEM)] * 3,
        scratch_shapes=[
            vmem((lists, depth), BF16),
            vmem((rows, depth), BF16),
            vmem((lists, rows), F32),
            vmem((16, depth // 16, rows), BF16),
            vmem((lists, rows), BF16),
            vmem((groups, 4, 16, part, 128), F32),
            vmem((groups, 4, 8, part, 128), F32),
            vmem((groups, 4, 4, part, 128), F32),
            vmem((groups, 4, 2, part, 128), F32),
            vmem((groups, 4, 1, part, 128), F32),
            vmem((lists, 128), F32),
            vmem((lists, 128), F32),
            vmem((ITERS + 1, ncol, 128), F32),
            vmem((ITERS + 1, 15, ncol, 128), F32),
            vmem((ITERS, nrow, 128), F32),
            vmem((ITERS, nrow, 128), F32),
            vmem((ITERS, nrow, 128), F32),
            vmem((ITERS, 7, nrow, 128), F32),
            vmem((nrow, 128), F32),
            vmem((nrow, 128), F32),
            vmem((nrow, 128), F32),
            dma((1 + rows // CHUNK,)),
            dma, dma((ITERS + 1,)),
            dma, dma((ITERS,)),
            dma, dma((ITERS,)),
            dma((4,)), dma((groups, 4, 4)),
        ],
        compiler_params=pltpu.CompilerParams(
            collective_id=0, has_side_effects=True, vmem_limit_bytes=56 << 20
        ),
        cost_estimate=pl.CostEstimate(
            flops=4 * rows * depth * lists, bytes_accessed=2 * (rows + lists) * depth,
            transcendentals=2 * rows * lists,
        ),
    )(passages, centroids)
    return out, cp.reshape(lists), rp.reshape(rows)


def solution(mesh):
    return jax.shard_map(
        functools.partial(local, mesh.shape["pass"], mesh.shape["list"]),
        mesh=mesh,
        in_specs=(P("pass", None), P("list", None)),
        out_specs=(P("pass", "list"), P("list"), P("pass")),
        check_vma=False,
    )
```

time: 848 us -> 102 us (0.12)
  blocking collectives: 698 us -> 0 us
  Pallas kernels: 0 us -> 96.5 us
  other arithmetic: 74.3 us -> 0 us
  waiting for transfers between devices: 37.7 us -> 0 us
  matrix products: 17.9 us -> 0 us
  between operations: 14.2 us -> 0.64 us
    psum x9 -> x0, blocking collectives: 363 us -> none  [the longest x4 183 us: row_lse(): total = lax.psum(jnp.sum(jnp.exp(moved - top[:, None]), axis=1), 'list')]
    pmax x8 -> x0, blocking collectives: 336 us -> none  [the longest x4 182 us: row_lse(): top = lax.pmax(local_max, 'list')]
    pallas_call x0 -> x1, Pallas kernels: none -> 96.5 us  [local(): pl.pallas_call(functools.partial(kernel, share), out_shape=(jax.ShapeDtyp...]
    reduce_sum x9 -> x0, other arithmetic: 43.4 us -> none  [the longest x4 19.7 us: row_lse(): total = lax.psum(jnp.sum(jnp.exp(moved - top[:, None]), axis=1), 'list')]
    unnamed x2 -> x0, waiting for transfers between devices: 37.7 us -> none
    reduce_max x7 -> x0, other arithmetic: 30.6 us -> none  [the longest x4 17.5 us: row_lse(): local_max = jnp.max(moved, axis=1)]
    dot_general x2 -> x0, matrix products: 17.9 us -> none  [the longest x1 9.27 us: local(): lax.dot_general(passages, weights, (((0,), (0,)), ((), ())), preferred_el...]
  transfers between devices with their start and end apart: 1 -> 0, of which waited for: 1 -> 0; matrix products, arithmetic and copies ran while one was open for 1% -> 0% of each run, Pallas kernels for 0% -> 0%
where the time goes in v1:
time: 102 us; the launch traced here: 101 us
  Pallas kernels  96.5 us (95%)
  local copies, waits for them, and re-layouts  4.16 us (4%)
    pallas_call x1, Pallas kernels, local(): pl.pallas_call(functools.partial(kernel, share), out_shape=(jax.ShapeDtyp...  96.5 us
    unnamed x3, local copies, waits for them, and re-layouts  4.16 us

profile of v1, /device:TPU:32, one launch (start us, length us, event | category | flops | bytes accessed | tf_op | source)
XLA Modules:
  0.0 101.3 jit_solution(5460074684866159400)
XLA Ops:
  0.6 96.5 %shard_map.49 = (f32[48,768]{1,0:T(8,128)}, f32[6,128]{1,0:T(8,128)}, f32[24,128]{1,0:T(8,128)}) custom-call(bf16[3072,768]{1,0:T(8,128)(2,1)} %pas_hbm.1, bf16[768,768]{1,0:T(8,128)(2,1)} %cen_hbm.1), custom_call_target="tpu_custom_call" | custom-call | flops 7247757312 | bytes 5898240 | tf_op jit(solution)/shard_map/pallas_call | solution.py:311
  97.1 1.6 %copy.8 = f32[48,768]{1,0:T(8,128)} copy(f32[48,768]{1,0:T(8,128)} %get-tuple-element.12) | data formatting | bytes 294912
  98.7 1.3 %copy.9 = f32[768]{0:T(1024)} copy(f32[768]{0:T(1024)} %bitcast.3) | data formatting | bytes 6144
  99.9 1.3 %copy.10 = f32[3072]{0:T(1024)} copy(f32[3072]{0:T(1024)} %bitcast.2) | data formatting | bytes 24576

commit v2 on v0

v2 whole, which is shorter than its diff:
```python
import functools
import math

import jax
import jax.numpy as jnp
from jax import lax
from jax.experimental import pallas as pl
from jax.experimental.pallas import tpu as pltpu
from jax.sharding import PartitionSpec as P

ITERS = 4
INV_TEMP = 20.0
LOG2E = math.log2(math.e)
LN2 = math.log(2.0)
F32 = jnp.float32
BF16 = jnp.bfloat16
MESH = pl.DeviceIdType.MESH
CHUNK = 512
GROUP = 256
STEP = 4
NA = 16
LINKS = (4, 12, 1, 3)
ORDERS = ((0, 1, 2, 3), (1, 0, 3, 2), (2, 3, 0, 1), (3, 2, 1, 0))


def flip(index, bits):
    out = index
    b = 1
    while b <= bits:
        if bits & b:
            out = out + b * (1 - 2 * ((index // b) % 2))
        b *= 2
    return out


def place_of(order):
    first = order[0]
    axis_bits = lambda seq, unit: [0, unit * seq[1], unit * seq[0], unit * (seq[0] ^ seq[1])]
    low = {0: 1, 1: 3, 2: 1, 3: 3}
    unit = {0: 4, 1: 4, 2: 1, 3: 1}
    major = axis_bits((low[order[0]], low[order[1]]), unit[first])
    minor = axis_bits((low[order[2]], low[order[3]]), unit[order[2]])
    return [a + b for a in major for b in minor]


PLACES = [place_of(order) for order in ORDERS]


def tree(values, op):
    while len(values) > 1:
        values = [op(values[i], values[i + 1]) for i in range(0, len(values), 2)]
    return values[0]


def lse2(values):
    top = tree(values, jnp.maximum)
    total = tree([jnp.exp2(v - top) for v in values], lax.add)
    return top + jnp.log(total) * LOG2E


def ring_hops(bits, size):
    return max(min(abs((i ^ bits) - i), size - abs((i ^ bits) - i)) for i in range(size))


PASS_ORDER = sorted(range(1, 16), key=lambda k: -ring_hops(k // 4, 4) - ring_hops(k % 4, 4))
Z_ORDER = sorted(range(1, 8), key=lambda k: -ring_hops(k, 8))
LIST_ORDER = sorted(range(1, 16), key=lambda k: -ring_hops(k // 2, 8))


def kernel(
    share, na,
    pas_hbm, cen_hbm,
    out_ref, cp_ref, rp_ref,
    cen, pas, tile, gain, pas_t, wts, stag, rb0, rb1, rb2, rb3,
    lane_a, lane_b, lane_c, racc, csrc, cslot, asrc, apair, amid, aslot, bsrc, bslot,
    u_ref, w_ref, m_ref, cfac, in_sem, cs, cr, ps, pr, zs, zr, bs, br, ss, sr,
):
    rows, depth = pas.shape
    lists = cen.shape[0]
    nrow, ncol = rows // 128, lists // 128
    nhalf = ncol // 2
    p, l = lax.axis_index("pass"), lax.axis_index("list")
    rbs = (rb0, rb1, rb2, rb3)
    add = lambda values: tree(values, lax.add)

    loads = [pltpu.make_async_copy(cen_hbm, cen, in_sem.at[0])]
    for b in range(rows // CHUNK):
        part = pl.ds(b * CHUNK, CHUNK)
        loads.append(pltpu.make_async_copy(pas_hbm.at[part], pas.at[part], in_sem.at[b + 1]))
    for load in loads:
        load.start()

    barrier = pltpu.get_barrier_semaphore()
    for k in PASS_ORDER:
        pl.semaphore_signal(barrier, inc=1, device_id=(flip(p, k), l), device_id_type=MESH)
    for k in LIST_ORDER:
        pl.semaphore_signal(barrier, inc=1, device_id=(p, flip(l, k)), device_id_type=MESH)

    def col_send(i, h):
        for k in PASS_ORDER:
            pltpu.make_async_remote_copy(
                src_ref=csrc.at[i, h], dst_ref=cslot.at[i, h, k - 1], send_sem=cs,
                recv_sem=cr.at[i, h], device_id=(flip(p, k), l), device_id_type=MESH,
            ).start()

    def col_recv(i, h):
        pltpu.make_async_copy(cslot.at[i, h], cslot.at[i, h], cr.at[i, h]).wait()
        return [csrc[i, h]] + [cslot[i, h, k] for k in range(15)]

    def a_pair(i):
        return pltpu.make_async_remote_copy(
            src_ref=asrc.at[i], dst_ref=apair.at[i], send_sem=ps, recv_sem=pr.at[i],
            device_id=(p, flip(l, 1)), device_id_type=MESH,
        )

    def a_send(i, combine):
        a_pair(i).wait_recv()
        amid[i] = combine([asrc[i], apair[i]])
        for k in Z_ORDER:
            pltpu.make_async_remote_copy(
                src_ref=amid.at[i], dst_ref=aslot.at[i, k - 1], send_sem=zs, recv_sem=zr.at[i],
                device_id=(p, flip(l, 2 * k)), device_id_type=MESH,
            ).start()

    def a_recv(i, combine):
        pltpu.make_async_copy(aslot.at[i], aslot.at[i], zr.at[i]).wait()
        return combine([amid[i]] + [aslot[i, k] for k in range(7)])

    def b_send(i):
        for k in LIST_ORDER:
            pltpu.make_async_remote_copy(
                src_ref=bsrc.at[i], dst_ref=bslot.at[i, k - 1], send_sem=bs, recv_sem=br.at[i],
                device_id=(p, flip(l, k)), device_id_type=MESH,
            ).start()

    def b_recv(i, combine):
        pltpu.make_async_copy(bslot.at[i], bslot.at[i], br.at[i]).wait()
        return combine([bsrc[i]] + [bslot[i, k] for k in range(15)])

    def loop(first, last, body):
        def step(i, carry):
            body(i)
            return carry

        lax.fori_loop(first, last, step, 0)

    def unrolled(first, last, body):
        for i in range(first, last):
            body(i)

    def send_rows(i, combine, sweep):
        def part(ref, first):
            def body(b):
                for c, value in enumerate(sweep(b)):
                    ref[i, b * STEP + c - first:b * STEP + c - first + 1, :] = value

            return body

        unrolled(0, na // STEP, part(asrc, 0))
        a_pair(i).start()
        unrolled(na // STEP, nrow // STEP, part(bsrc, na))
        b_send(i)
        a_send(i, combine)

    part_a, part_b = slice(0, na), slice(na, nrow)

    def spread(values, h):
        for k in range(nhalf):
            at = pl.multiple_of((h * nhalf + k) * 128, 128)
            lane_b[pl.ds(at, 128), :] = jnp.broadcast_to(values[k:k + 1, :], (128, 128)).T

    def fold(i, h, ref):
        for k in range(nhalf):
            at = pl.multiple_of((h * nhalf + k) * 128, 128)
            csrc[i, h, k:k + 1, :] = jnp.sum(ref[pl.ds(at, 128), :].T, axis=0, keepdims=True)

    loads[0].wait()

    def logits(b):
        part = pl.ds(pl.multiple_of(b * CHUNK, CHUNK), CHUNK)
        pltpu.make_async_copy(pas_hbm.at[part], pas.at[part], in_sem.at[b + 1]).wait()
        tile[:, part] = lax.dot_general(
            cen[...], pas[part, :], (((1,), (1,)), ((), ())), preferred_element_type=F32
        ) * (INV_TEMP * LOG2E)

    loop(0, rows // CHUNK, logits)

    def col_first(h):
        def body(r, carry):
            base = pl.ds(pl.multiple_of(h * lists // 2 + r * 8, 8), 8)
            parts = [tile[base, c * 128:(c + 1) * 128] for c in range(nrow)]
            top = functools.reduce(jnp.maximum, parts)
            lane_a[base, :] = top
            lane_b[base, :] = functools.reduce(lax.add, [jnp.exp2(part - top) for part in parts])
            return carry

        lax.fori_loop(0, lists // 16, body, 0, unroll=2)
        for k in range(nhalf):
            at = pl.ds(pl.multiple_of((h * nhalf + k) * 128, 128), 128)
            tops = lane_a[at, :].T
            sums = lane_b[at, :].T
            top = jnp.max(tops, axis=0, keepdims=True)
            total = jnp.sum(sums * jnp.exp2(tops - top), axis=0, keepdims=True)
            csrc[0, h, k:k + 1, :] = top + jnp.log(total) * LOG2E
        col_send(0, h)

    pl.semaphore_wait(barrier, 30)
    loop(0, 2, col_first)

    def turn(b):
        part = pl.ds(pl.multiple_of(b * CHUNK, CHUNK), CHUNK)
        pas_t[:, :, part] = pas[part, :].T.reshape(16, depth // 16, CHUNK)

    loop(0, rows // CHUNK, turn)
    for h in range(2):
        col_pot = share * LOG2E - lse2(col_recv(0, h))
        cp_ref[h * nhalf:(h + 1) * nhalf, :] = col_pot * LN2
        spread(col_pot, h)

    def columns(b):
        return [slice((b * STEP + c) * 128, (b * STEP + c + 1) * 128) for c in range(STEP)]

    def row_first(b):
        cols = columns(b)

        def row_top(r, tops):
            out = []
            for j in range(2):
                base = pl.ds(pl.multiple_of(r * 16, 16) + 8 * j, 8)
                pot = lane_b[base, :]
                out += [jnp.maximum(top, tile[base, col] + pot)
                        for top, col in zip(tops[j * STEP:(j + 1) * STEP], cols)]
            return tuple(out)

        tops = lax.fori_loop(
            0, lists // 16, row_top,
            tuple(jnp.full((8, 128), -jnp.inf, F32) for _ in range(2 * STEP)), unroll=4,
        )
        tops = [jnp.max(jnp.maximum(tops[c], tops[c + STEP]), axis=0, keepdims=True) for c in range(STEP)]
        wide = [jnp.broadcast_to(top, (8, 128)) for top in tops]

        def row_exp(r, sums):
            out = []
            for j in range(2):
                base = pl.ds(pl.multiple_of(r * 16, 16) + 8 * j, 8)
                pot = lane_b[base, :]
                for total, col, top in zip(sums[j * STEP:(j + 1) * STEP], cols, wide):
                    e = jnp.exp2(tile[base, col] + pot - top)
                    gain[base, col] = e
                    out.append(total + e)
            return tuple(out)

        sums = lax.fori_loop(
            0, lists // 16, row_exp, tuple(jnp.zeros((8, 128), F32) for _ in range(2 * STEP)), unroll=4
        )
        result = []
        for c, top in enumerate(tops):
            total = jnp.sum(sums[c] + sums[c + STEP], axis=0, keepdims=True)
            m_ref[pl.ds(b * STEP + c, 1), :] = top
            result.append(top + jnp.log(total) * LOG2E)
        return result

    send_rows(0, lse2, row_first)

    def first_factors(part, row_pot):
        rp_ref[part, :] = row_pot * LN2
        w_ref[part, :] = jnp.exp2(m_ref[part, :] + row_pot)
        u_ref[part, :] = w_ref[part, :]

    def next_factors(part, row_fac):
        u_ref[part, :] = w_ref[part, :] * row_fac
        m_ref[part, :] = row_fac

    def factors(part):
        return [jnp.broadcast_to(u_ref[c:c + 1, :], (8, 128)) for c in range(part.start, part.stop)]

    def col_sweep(part, first, count, out, start):
        us = factors(part)

        def body(r, carry):
            base = pl.ds(pl.multiple_of(first + r * 8, 8), 8)
            total = tree_sum([gain[base, c * 128:(c + 1) * 128] * us[c - part.start]
                              for c in range(part.start, part.stop)])
            out[base, :] = total if start is None else total + start[base, :]
            return carry

        lax.fori_loop(0, count // 8, body, 0, unroll=4)

    def row_sweep(b, h):
        cols = columns(b)

        def body(r, sums):
            out = []
            for j in range(2):
                base = pl.ds(pl.multiple_of(h * lists // 2 + r * 16, 16) + 8 * j, 8)
                fac = lane_b[base, :]
                out += [total + gain[base, col] * fac
                        for total, col in zip(sums[j * STEP:(j + 1) * STEP], cols)]
            return tuple(out)

        sums = lax.fori_loop(
            0, lists // 32, body, tuple(jnp.zeros((8, 128), F32) for _ in range(2 * STEP)), unroll=4
        )
        return [sums[c] + sums[c + STEP] for c in range(STEP)], cols

    def plan(part, first, count, out, start):
        us = factors(part)

        def body(r):
            base = pl.multiple_of(first + r * 16, 16)
            low, high = pl.ds(base, 8), pl.ds(base + 8, 8)
            fac_low, fac_high = lane_b[low, :], lane_b[high, :]
            sums_low, sums_high = [], []
            for c in range(part.start, part.stop):
                col = slice(c * 128, (c + 1) * 128)
                a = gain[low, col] * us[c - part.start] * fac_low
                b = gain[high, col] * us[c - part.start] * fac_high
                sums_low.append(a)
                sums_high.append(b)
                wts[pl.ds(base, 16), col] = jnp.concatenate([a, b], axis=0).astype(BF16)
            sum_low, sum_high = tree_sum(sums_low), tree_sum(sums_high)
            out[low, :] = sum_low if start is None else sum_low + start[low, :]
            out[high, :] = sum_high if start is None else sum_high + start[high, :]

        loop(0, count // 16, body)

    first_factors(part_b, -b_recv(0, lse2))
    col_sweep(part_b, 0, lists, lane_a, None)
    first_factors(part_a, -a_recv(0, lse2))

    def iteration(step):
        def col_half(h):
            col_sweep(part_a, h * lists // 2, lists // 2, lane_c, lane_a)
            fold(step, h, lane_c)
            col_send(step, h)

        loop(0, 2, col_half)
        for h in range(2):
            col_fac = math.exp(share) / add(col_recv(step, h))
            cfac[h] = col_fac
            spread(col_fac, h)
            if h == 0:
                def first_half(b):
                    sums, cols = row_sweep(b, 0)
                    for total, col in zip(sums, cols):
                        racc[:, col] = total

                unrolled(0, nrow // STEP, first_half)

        def last_half(b):
            sums, cols = row_sweep(b, 1)
            return [
                jnp.sum(total + racc[:, col], axis=0, keepdims=True) * w_ref[pl.ds(b * STEP + c, 1), :]
                for c, (total, col) in enumerate(zip(sums, cols))
            ]

        send_rows(step, add, last_half)
        next_factors(part_b, 1.0 / b_recv(step, add))

        @pl.when(step < ITERS - 1)
        def _():
            col_sweep(part_b, 0, lists, lane_a, None)

        @pl.when(step == ITERS - 1)
        def _():
            plan(part_b, 0, lists, lane_a, None)

        next_factors(part_a, 1.0 / a_recv(step, add))

    loop(1, ITERS, iteration)

    half = depth // 32
    groups = lists // GROUP

    def hop(g, v, s):
        n = 8 >> s
        return pltpu.make_async_remote_copy(
            src_ref=stag.at[g, v, pl.ds(n, n)], dst_ref=rbs[s].at[g, v], send_sem=ss.at[s],
            recv_sem=sr.at[g, v, s], device_id=(flip(p, LINKS[ORDERS[v][s]]), l), device_id_type=MESH,
        )

    def group_sums(g):
        first = pl.multiple_of(g * GROUP, GROUP)
        plan(part_a, first, GROUP, lane_c, lane_a)
        w = wts[pl.ds(first, GROUP), :]
        left = jnp.concatenate([pas_t[flip(p, i)] for i in range(16)], axis=0)
        res = lax.dot_general(left, w, (((1,), (1,)), ((), ())), preferred_element_type=F32)
        for v in range(4):
            h, c = v // 2, v % 2
            for i in range(16):
                stag[g, v, PLACES[v].index(i)] = res[
                    (2 * i + h) * half:(2 * i + h + 1) * half, c * 128:(c + 1) * 128]
        for v in range(4):
            hop(g, v, 0).start()

    loop(0, groups, group_sums)

    def mass_half(h):
        fold(ITERS, h, lane_c)
        col_send(ITERS, h)

    loop(0, 2, mass_half)
    rp_ref[...] += jnp.log(m_ref[...])
    for h in range(2):
        cp_ref[h * nhalf:(h + 1) * nhalf, :] += jnp.log(cfac[h])
    for s in range(1, 4):
        def reduce(g, s=s):
            n = 16 >> s
            for v in range(4):
                hop(g, v, s - 1).wait_recv()
                for i in range(n // 2, n):
                    stag[g, v, i] += rbs[s - 1][g, v, i]
                hop(g, v, s).start()
                for i in range(n // 2):
                    stag[g, v, i] += rbs[s - 1][g, v, i]

        loop(0, groups, reduce)
    mass = [add(col_recv(ITERS, h)) for h in range(2)]
    for g in range(groups):
        for v in range(4):
            hop(g, v, 3).wait_recv()
            h, c = v // 2, v % 2
            at = g * (GROUP // 128) + c
            out_ref[h * half:(h + 1) * half, at * 128:(at + 1) * 128] = (
                stag[g, v, 0] + rb3[g, v, 0]) / mass[at // nhalf][at % nhalf:at % nhalf + 1, :]

    for ref, sem in ((cslot, cs), (apair, ps), (aslot, zs), (bslot, bs)):
        pltpu.make_async_copy(ref, ref, sem).wait()
    for s in range(4):
        pltpu.make_async_copy(rbs[s], rbs[s], ss.at[s]).wait()


def copy_out(*refs):
    n = len(refs) // 2
    for src, dst in zip(refs[:n], refs[n:]):
        dst[...] = src[...]


def tree_sum(values):
    values = list(values)
    while len(values) > 1:
        pairs = [values[i] + values[i + 1] for i in range(0, len(values) - 1, 2)]
        values = pairs + values[len(values) - len(values) % 2:]
    return values[0]


def local(n_pass, n_list, passages, centroids):
    rows, depth = passages.shape
    lists = centroids.shape[0]
    nrow, ncol = rows // 128, lists // 128
    na = NA
    share = math.log(rows * n_pass / (lists * n_list))
    groups, part = lists // GROUP, depth // 32
    dma = pltpu.SemaphoreType.DMA
    vmem = pltpu.VMEM
    shapes = (
        jax.ShapeDtypeStruct((depth // n_pass, lists), F32),
        jax.ShapeDtypeStruct((ncol, 128), F32),
        jax.ShapeDtypeStruct((nrow, 128), F32),
    )
    whole = pl.BlockSpec(memory_space=pltpu.VMEM)
    results = pl.pallas_call(
        functools.partial(kernel, share, na),
        out_shape=shapes,
        in_specs=[pl.BlockSpec(memory_space=pl.ANY)] * 2,
        out_specs=[whole] * 3,
        scratch_shapes=[
            vmem((lists, depth), BF16),
            vmem((rows, depth), BF16),
            vmem((lists, rows), F32),
            vmem((lists, rows), F32),
            vmem((16, depth // 16, rows), BF16),
            vmem((lists, rows), BF16),
            vmem((groups, 4, 16, part, 128), F32),
            vmem((groups, 4, 8, part, 128), F32),
            vmem((groups, 4, 4, part, 128), F32),
            vmem((groups, 4, 2, part, 128), F32),
            vmem((groups, 4, 1, part, 128), F32),
            vmem((lists, 128), F32),
            vmem((lists, 128), F32),
            vmem((lists, 128), F32),
            vmem((8, rows), F32),
            vmem((ITERS + 1, 2, ncol // 2, 128), F32),
            vmem((ITERS + 1, 2, 15, ncol // 2, 128), F32),
            vmem((ITERS, na, 128), F32),
            vmem((ITERS, na, 128), F32),
            vmem((ITERS, na, 128), F32),
            vmem((ITERS, 7, na, 128), F32),
            vmem((ITERS, nrow - na, 128), F32),
            vmem((ITERS, 15, nrow - na, 128), F32),
            vmem((nrow, 128), F32),
            vmem((nrow, 128), F32),
            vmem((nrow, 128), F32),
            vmem((2, ncol // 2, 128), F32),
            dma((1 + rows // CHUNK,)),
            dma, dma((ITERS + 1, 2)),
            dma, dma((ITERS,)),
            dma, dma((ITERS,)),
            dma, dma((ITERS,)),
            dma((4,)), dma((groups, 4, 4)),
        ],
        compiler_params=pltpu.CompilerParams(
            collective_id=0, has_side_effects=True, vmem_limit_bytes=56 << 20
        ),
        cost_estimate=pl.CostEstimate(
            flops=4 * rows * depth * lists, bytes_accessed=2 * (rows + lists) * depth,
            transcendentals=2 * rows * lists,
        ),
    )(passages, centroids)
    out, cp, rp = pl.pallas_call(
        copy_out, out_shape=shapes, in_specs=[whole] * 3, out_specs=[whole] * 3
    )(*results)
    return out, cp.reshape(lists), rp.reshape(rows)


def solution(mesh):
    return jax.shard_map(
        functools.partial(local, mesh.shape["pass"], mesh.shape["list"]),
        mesh=mesh,
        in_specs=(P("pass", None), P("list", None)),
        out_specs=(P("pass", "list"), P("list"), P("pass")),
        check_vma=False,
    )
```

time: 848 us -> 90.9 us (0.11)
  blocking collectives: 698 us -> 0 us
  Pallas kernels: 0 us -> 89.7 us
  other arithmetic: 74.3 us -> 0 us
  waiting for transfers between devices: 37.7 us -> 0 us
  matrix products: 17.9 us -> 0 us
  between operations: 14.2 us -> 0.64 us
    psum x9 -> x0, blocking collectives: 363 us -> none  [the longest x4 183 us: row_lse(): total = lax.psum(jnp.sum(jnp.exp(moved - top[:, None]), axis=1), 'list')]
    pmax x8 -> x0, blocking collectives: 336 us -> none  [the longest x4 182 us: row_lse(): top = lax.pmax(local_max, 'list')]
    pallas_call x0 -> x2, Pallas kernels: none -> 89.7 us  [the longest x1 88.1 us: local(): pl.pallas_call(functools.partial(kernel, share, na), out_shape=shapes, in...]
    reduce_sum x9 -> x0, other arithmetic: 43.4 us -> none  [the longest x4 19.7 us: row_lse(): total = lax.psum(jnp.sum(jnp.exp(moved - top[:, None]), axis=1), 'list')]
    unnamed x2 -> x0, waiting for transfers between devices: 37.7 us -> none
    reduce_max x7 -> x0, other arithmetic: 30.6 us -> none  [the longest x4 17.5 us: row_lse(): local_max = jnp.max(moved, axis=1)]
    dot_general x2 -> x0, matrix products: 17.9 us -> none  [the longest x1 9.27 us: local(): lax.dot_general(passages, weights, (((0,), (0,)), ((), ())), preferred_el...]
  transfers between devices with their start and end apart: 1 -> 0, of which waited for: 1 -> 0; matrix products, arithmetic and copies ran while one was open for 1% -> 0% of each run, Pallas kernels for 0% -> 0%
where the time goes in v2:
time: 90.9 us; the launch traced here: 90.4 us
  Pallas kernels  89.7 us (99%)
    pallas_call x1, Pallas kernels, local(): pl.pallas_call(functools.partial(kernel, share, na), out_shape=shapes, in...  88.1 us

profile of v2, /device:TPU:32, one launch (start us, length us, event | category | flops | bytes accessed | tf_op | source)
XLA Modules:
  0.0 90.4 jit_solution(11788964814971585821)
XLA Ops:
  0.6 88.1 %shard_map.49 = (f32[48,768]{1,0:T(8,128)}, f32[6,128]{1,0:T(8,128)}, f32[24,128]{1,0:T(8,128)}) custom-call(bf16[3072,768]{1,0:T(8,128)(2,1)} %pas_hbm.1, bf16[768,768]{1,0:T(8,128)(2,1)} %cen_hbm.1), custom_call_target="tpu_custom_call" | custom-call | flops 7247757312 | bytes 5898240 | tf_op jit(solution)/shard_map/pallas_call | solution.py:462
  88.8 1.6 %shard_map.50 = (f32[48,768]{1,0:T(8,128)}, f32[6,128]{1,0:T(8,128)}, f32[24,128]{1,0:T(8,128)}) custom-call(f32[48,768]{1,0:T(8,128)} %get-tuple-element.9.refs_0_, f32[6,128]{1,0:T(8,128)} %get-tuple-element.10.refs_1_, f32[24,128]{1,0:T(8,128)} %get-tuple-element.11.refs_2_), custom_call_target="tpu_custom_call" | custom-call | tf_op jit(solution)/shard_map/pallas_call | solution.py:510

commit v3 on v2

--- a/solution.py
+++ b/solution.py
@@ -19,6 +19,8 @@
 GROUP = 256
 STEP = 4
 NA = 16
+PARTS = 1
+LAST_ORDER = (3, 2, 1)
 LINKS = (4, 12, 1, 3)
 ORDERS = ((0, 1, 2, 3), (1, 0, 3, 2), (2, 3, 0, 1), (3, 2, 1, 0))
 
@@ -46,6 +48,13 @@
 PLACES = [place_of(order) for order in ORDERS]
 
 
+def chains(values, op, count=4):
+    heads = list(values[:count])
+    for i, value in enumerate(values[count:]):
+        heads[i % count] = op(heads[i % count], value)
+    return tree(heads, op)
+
+
 def tree(values, op):
     while len(values) > 1:
         values = [op(values[i], values[i + 1]) for i in range(0, len(values), 2)]
@@ -71,16 +80,15 @@
     share, na,
     pas_hbm, cen_hbm,
     out_ref, cp_ref, rp_ref,
-    cen, pas, tile, gain, pas_t, wts, stag, rb0, rb1, rb2, rb3,
+    cen, pas, tile, gain, pas_t, wts, stag, rb0, rb1, rb2,
     lane_a, lane_b, lane_c, racc, csrc, cslot, asrc, apair, amid, aslot, bsrc, bslot,
     u_ref, w_ref, m_ref, cfac, in_sem, cs, cr, ps, pr, zs, zr, bs, br, ss, sr,
 ):
     rows, depth = pas.shape
     lists = cen.shape[0]
     nrow, ncol = rows // 128, lists // 128
-    nhalf = ncol // 2
+    nhalf = ncol // PARTS
     p, l = lax.axis_index("pass"), lax.axis_index("list")
-    rbs = (rb0, rb1, rb2, rb3)
     add = lambda values: tree(values, lax.add)
 
     loads = [pltpu.make_async_copy(cen_hbm, cen, in_sem.at[0])]
@@ -187,14 +195,14 @@
 
     def col_first(h):
         def body(r, carry):
-            base = pl.ds(pl.multiple_of(h * lists // 2 + r * 8, 8), 8)
+            base = pl.ds(pl.multiple_of(h * (lists // PARTS) + r * 8, 8), 8)
             parts = [tile[base, c * 128:(c + 1) * 128] for c in range(nrow)]
-            top = functools.reduce(jnp.maximum, parts)
+            top = chains(parts, jnp.maximum)
             lane_a[base, :] = top
-            lane_b[base, :] = functools.reduce(lax.add, [jnp.exp2(part - top) for part in parts])
+            lane_b[base, :] = chains([jnp.exp2(part - top) for part in parts], lax.add)
             return carry
 
-        lax.fori_loop(0, lists // 16, body, 0, unroll=2)
+        lax.fori_loop(0, lists // (8 * PARTS), body, 0, unroll=4)
         for k in range(nhalf):
             at = pl.ds(pl.multiple_of((h * nhalf + k) * 128, 128), 128)
             tops = lane_a[at, :].T
@@ -205,14 +213,14 @@
         col_send(0, h)
 
     pl.semaphore_wait(barrier, 30)
-    loop(0, 2, col_first)
+    loop(0, PARTS, col_first)
 
     def turn(b):
         part = pl.ds(pl.multiple_of(b * CHUNK, CHUNK), CHUNK)
         pas_t[:, :, part] = pas[part, :].T.reshape(16, depth // 16, CHUNK)
 
     loop(0, rows // CHUNK, turn)
-    for h in range(2):
+    for h in range(PARTS):
         col_pot = share * LOG2E - lse2(col_recv(0, h))
         cp_ref[h * nhalf:(h + 1) * nhalf, :] = col_pot * LN2
         spread(col_pot, h)
@@ -292,14 +300,14 @@
         def body(r, sums):
             out = []
             for j in range(2):
-                base = pl.ds(pl.multiple_of(h * lists // 2 + r * 16, 16) + 8 * j, 8)
+                base = pl.ds(pl.multiple_of(h * (lists // PARTS) + r * 16, 16) + 8 * j, 8)
                 fac = lane_b[base, :]
                 out += [total + gain[base, col] * fac
                         for total, col in zip(sums[j * STEP:(j + 1) * STEP], cols)]
             return tuple(out)
 
         sums = lax.fori_loop(
-            0, lists // 32, body, tuple(jnp.zeros((8, 128), F32) for _ in range(2 * STEP)), unroll=4
+            0, lists // (16 * PARTS), body, tuple(jnp.zeros((8, 128), F32) for _ in range(2 * STEP)), unroll=4
         )
         return [sums[c] + sums[c + STEP] for c in range(STEP)], cols
 
@@ -330,16 +338,16 @@
 
     def iteration(step):
         def col_half(h):
-            col_sweep(part_a, h * lists // 2, lists // 2, lane_c, lane_a)
+            col_sweep(part_a, h * (lists // PARTS), lists // PARTS, lane_c, lane_a)
             fold(step, h, lane_c)
             col_send(step, h)
 
-        loop(0, 2, col_half)
-        for h in range(2):
+        loop(0, PARTS, col_half)
+        for h in range(PARTS):
             col_fac = math.exp(share) / add(col_recv(step, h))
             cfac[h] = col_fac
             spread(col_fac, h)
-            if h == 0:
+            if h < PARTS - 1:
                 def first_half(b):
                     sums, cols = row_sweep(b, 0)
                     for total, col in zip(sums, cols):
@@ -348,9 +356,9 @@
                 unrolled(0, nrow // STEP, first_half)
 
         def last_half(b):
-            sums, cols = row_sweep(b, 1)
+            sums, cols = row_sweep(b, PARTS - 1)
             return [
-                jnp.sum(total + racc[:, col], axis=0, keepdims=True) * w_ref[pl.ds(b * STEP + c, 1), :]
+                jnp.sum(total + racc[:, col] if PARTS > 1 else total, axis=0, keepdims=True) * w_ref[pl.ds(b * STEP + c, 1), :]
                 for c, (total, col) in enumerate(zip(sums, cols))
             ]
 
@@ -375,7 +383,7 @@
     def hop(g, v, s):
         n = 8 >> s
         return pltpu.make_async_remote_copy(
-            src_ref=stag.at[g, v, pl.ds(n, n)], dst_ref=rbs[s].at[g, v], send_sem=ss.at[s],
+            src_ref=stag.at[g, v, pl.ds(n, n)], dst_ref=(rb0, rb1)[s].at[g, v], send_sem=ss.at[s],
             recv_sem=sr.at[g, v, s], device_id=(flip(p, LINKS[ORDERS[v][s]]), l), device_id_type=MESH,
         )
 
@@ -399,35 +407,46 @@
         fold(ITERS, h, lane_c)
         col_send(ITERS, h)
 
-    loop(0, 2, mass_half)
+    loop(0, PARTS, mass_half)
     rp_ref[...] += jnp.log(m_ref[...])
-    for h in range(2):
+    for h in range(PARTS):
         cp_ref[h * nhalf:(h + 1) * nhalf, :] += jnp.log(cfac[h])
-    for s in range(1, 4):
-        def reduce(g, s=s):
-            n = 16 >> s
-            for v in range(4):
-                hop(g, v, s - 1).wait_recv()
-                for i in range(n // 2, n):
-                    stag[g, v, i] += rbs[s - 1][g, v, i]
-                hop(g, v, s).start()
-                for i in range(n // 2):
-                    stag[g, v, i] += rbs[s - 1][g, v, i]
-
-        loop(0, groups, reduce)
-    mass = [add(col_recv(ITERS, h)) for h in range(2)]
+    def second(g):
+        for v in range(4):
+            hop(g, v, 0).wait_recv()
+            for i in range(4, 8):
+                stag[g, v, i] += rb0[g, v, i]
+            hop(g, v, 1).start()
+            for i in range(4):
+                stag[g, v, i] += rb0[g, v, i]
+
+    def third(g):
+        for v in range(4):
+            hop(g, v, 1).wait_recv()
+            for i in LAST_ORDER:
+                stag[g, v, i] += rb1[g, v, i]
+                pltpu.make_async_remote_copy(
+                    src_ref=stag.at[g, v, i], dst_ref=rb2.at[g, v, i - 1], send_sem=ss.at[2],
+                    recv_sem=sr.at[g, v, 2], device_id=(flip(p, PLACES[v][i]), l), device_id_type=MESH,
+                ).start()
+            stag[g, v, 0] += rb1[g, v, 0]
+
+    loop(0, groups, second)
+    loop(0, groups, third)
+    mass = [add(col_recv(ITERS, h)) for h in range(PARTS)]
     for g in range(groups):
         for v in range(4):
-            hop(g, v, 3).wait_recv()
+            pltpu.make_async_copy(rb2.at[g, v], rb2.at[g, v], sr.at[g, v, 2]).wait()
             h, c = v // 2, v % 2
             at = g * (GROUP // 128) + c
+            total = (stag[g, v, 0] + rb2[g, v, 0]) + (rb2[g, v, 1] + rb2[g, v, 2])
             out_ref[h * half:(h + 1) * half, at * 128:(at + 1) * 128] = (
-                stag[g, v, 0] + rb3[g, v, 0]) / mass[at // nhalf][at % nhalf:at % nhalf + 1, :]
+                total / mass[at // nhalf][at % nhalf:at % nhalf + 1, :])
 
     for ref, sem in ((cslot, cs), (apair, ps), (aslot, zs), (bslot, bs)):
         pltpu.make_async_copy(ref, ref, sem).wait()
-    for s in range(4):
-        pltpu.make_async_copy(rbs[s], rbs[s], ss.at[s]).wait()
+    for s, ref in enumerate((rb0, rb1, rb2)):
+        pltpu.make_async_copy(ref, ref, ss.at[s]).wait()
 
 
 def copy_out(*refs):
@@ -474,14 +493,13 @@
             vmem((groups, 4, 16, part, 128), F32),
             vmem((groups, 4, 8, part, 128), F32),
             vmem((groups, 4, 4, part, 128), F32),
-            vmem((groups, 4, 2, part, 128), F32),
-            vmem((groups, 4, 1, part, 128), F32),
+            vmem((groups, 4, 3, part, 128), F32),
             vmem((lists, 128), F32),
             vmem((lists, 128), F32),
             vmem((lists, 128), F32),
             vmem((8, rows), F32),
-            vmem((ITERS + 1, 2, ncol // 2, 128), F32),
-            vmem((ITERS + 1, 2, 15, ncol // 2, 128), F32),
+            vmem((ITERS + 1, PARTS, ncol // PARTS, 128), F32),
+            vmem((ITERS + 1, PARTS, 15, ncol // PARTS, 128), F32),
             vmem((ITERS, na, 128), F32),
             vmem((ITERS, na, 128), F32),
             vmem((ITERS, na, 128), F32),
@@ -491,13 +509,13 @@
             vmem((nrow, 128), F32),
             vmem((nrow, 128), F32),
             vmem((nrow, 128), F32),
-            vmem((2, ncol // 2, 128), F32),
+            vmem((PARTS, ncol // PARTS, 128), F32),
             dma((1 + rows // CHUNK,)),
-            dma, dma((ITERS + 1, 2)),
+            dma, dma((ITERS + 1, PARTS)),
             dma, dma((ITERS,)),
             dma, dma((ITERS,)),
             dma, dma((ITERS,)),
-            dma((4,)), dma((groups, 4, 4)),
+            dma((3,)), dma((groups, 4, 3)),
         ],
         compiler_params=pltpu.CompilerParams(
             collective_id=0, has_side_effects=True, vmem_limit_bytes=56 << 20

time: 90.9 us -> 87.8 us (0.966)
  Pallas kernels: 89.7 us -> 86.9 us
    pallas_call x1, Pallas kernels: 88.1 us -> 85.4 us  [local(): pl.pallas_call(functools.partial(kernel, share, na), out_shape=shapes, in...]
where the time goes in v3:
time: 87.8 us; the launch traced here: 87.6 us
  Pallas kernels  86.9 us (99%)
    pallas_call x1, Pallas kernels, local(): pl.pallas_call(functools.partial(kernel, share, na), out_shape=shapes, in...  85.4 us

profile of v3, /device:TPU:32, one launch (start us, length us, event | category | flops | bytes accessed | tf_op | source)
XLA Modules:
  0.0 87.6 jit_solution(17770259456793077011)
XLA Ops:
  0.6 85.4 %shard_map.49 = (f32[48,768]{1,0:T(8,128)}, f32[6,128]{1,0:T(8,128)}, f32[24,128]{1,0:T(8,128)}) custom-call(bf16[3072,768]{1,0:T(8,128)(2,1)} %pas_hbm.1, bf16[768,768]{1,0:T(8,128)(2,1)} %cen_hbm.1), custom_call_target="tpu_custom_call" | custom-call | flops 7247757312 | bytes 5898240 | tf_op jit(solution)/shard_map/pallas_call | solution.py:481
  86.0 1.6 %shard_map.50 = (f32[48,768]{1,0:T(8,128)}, f32[6,128]{1,0:T(8,128)}, f32[24,128]{1,0:T(8,128)}) custom-call(f32[48,768]{1,0:T(8,128)} %get-tuple-element.9.refs_0_, f32[6,128]{1,0:T(8,128)} %get-tuple-element.10.refs_1_, f32[24,128]{1,0:T(8,128)} %get-tuple-element.11.refs_2_), custom_call_target="tpu_custom_call" | custom-call | tf_op jit(solution)/shard_map/pallas_call | solution.py:528

commit v4 on v3

--- a/solution.py
+++ b/solution.py
@@ -17,7 +17,7 @@
 MESH = pl.DeviceIdType.MESH
 CHUNK = 512
 GROUP = 256
-STEP = 4
+STEP = 8
 NA = 16
 PARTS = 1
 LAST_ORDER = (3, 2, 1)
@@ -185,24 +185,35 @@
     loads[0].wait()
 
     def logits(b):
-        part = pl.ds(pl.multiple_of(b * CHUNK, CHUNK), CHUNK)
-        pltpu.make_async_copy(pas_hbm.at[part], pas.at[part], in_sem.at[b + 1]).wait()
+        part = slice(b * CHUNK, (b + 1) * CHUNK)
+        loads[b + 1].wait()
         tile[:, part] = lax.dot_general(
             cen[...], pas[part, :], (((1,), (1,)), ((), ())), preferred_element_type=F32
         ) * (INV_TEMP * LOG2E)
 
-    loop(0, rows // CHUNK, logits)
-
-    def col_first(h):
+    def col_first(b):
         def body(r, carry):
-            base = pl.ds(pl.multiple_of(h * (lists // PARTS) + r * 8, 8), 8)
-            parts = [tile[base, c * 128:(c + 1) * 128] for c in range(nrow)]
-            top = chains(parts, jnp.maximum)
+            base = pl.ds(pl.multiple_of(r * 8, 8), 8)
+            parts = [tile[base, c * 128:(c + 1) * 128] for c in range(b * CHUNK // 128, (b + 1) * CHUNK // 128)]
+            top = tree(parts, jnp.maximum)
+            if b > 0:
+                top = jnp.maximum(top, lane_a[base, :])
+            total = tree([jnp.exp2(part - top) for part in parts], lax.add)
+            if b > 0:
+                total = total + lane_b[base, :] * jnp.exp2(lane_a[base, :] - top)
             lane_a[base, :] = top
-            lane_b[base, :] = chains([jnp.exp2(part - top) for part in parts], lax.add)
+            lane_b[base, :] = total
             return carry
 
-        lax.fori_loop(0, lists // (8 * PARTS), body, 0, unroll=4)
+        lax.fori_loop(0, lists // 8, body, 0, unroll=96)
+
+    logits(0)
+    for b in range(1, rows // CHUNK):
+        logits(b)
+        col_first(b - 1)
+    col_first(rows // CHUNK - 1)
+
+    def col_first_send(h):
         for k in range(nhalf):
             at = pl.ds(pl.multiple_of((h * nhalf + k) * 128, 128), 128)
             tops = lane_a[at, :].T
@@ -213,7 +224,7 @@
         col_send(0, h)
 
     pl.semaphore_wait(barrier, 30)
-    loop(0, PARTS, col_first)
+    loop(0, PARTS, col_first_send)
 
     def turn(b):
         part = pl.ds(pl.multiple_of(b * CHUNK, CHUNK), CHUNK)
@@ -242,7 +253,7 @@
 
         tops = lax.fori_loop(
             0, lists // 16, row_top,
-            tuple(jnp.full((8, 128), -jnp.inf, F32) for _ in range(2 * STEP)), unroll=4,
+            tuple(jnp.full((8, 128), -jnp.inf, F32) for _ in range(2 * STEP)), unroll=8,
         )
         tops = [jnp.max(jnp.maximum(tops[c], tops[c + STEP]), axis=0, keepdims=True) for c in range(STEP)]
         wide = [jnp.broadcast_to(top, (8, 128)) for top in tops]
@@ -259,7 +270,7 @@
             return tuple(out)
 
         sums = lax.fori_loop(
-            0, lists // 16, row_exp, tuple(jnp.zeros((8, 128), F32) for _ in range(2 * STEP)), unroll=4
+            0, lists // 16, row_exp, tuple(jnp.zeros((8, 128), F32) for _ in range(2 * STEP)), unroll=8
         )
         result = []
         for c, top in enumerate(tops):
@@ -292,7 +303,7 @@
             out[base, :] = total if start is None else total + start[base, :]
             return carry
 
-        lax.fori_loop(0, count // 8, body, 0, unroll=4)
+        lax.fori_loop(0, count // 8, body, 0, unroll=8)
 
     def row_sweep(b, h):
         cols = columns(b)
@@ -307,7 +318,7 @@
             return tuple(out)
 
         sums = lax.fori_loop(
-            0, lists // (16 * PARTS), body, tuple(jnp.zeros((8, 128), F32) for _ in range(2 * STEP)), unroll=4
+            0, lists // (16 * PARTS), body, tuple(jnp.zeros((8, 128), F32) for _ in range(2 * STEP)), unroll=8
         )
         return [sums[c] + sums[c + STEP] for c in range(STEP)], cols
 

time: 87.8 us -> 83.6 us (0.952)
  Pallas kernels: 86.9 us -> 82.9 us
    pallas_call x1, Pallas kernels: 85.4 us -> 81.3 us  [local(): pl.pallas_call(functools.partial(kernel, share, na), out_shape=shapes, in...]
where the time goes in v4:
time: 83.6 us; the launch traced here: 83.5 us
  Pallas kernels  82.9 us (99%)
    pallas_call x1, Pallas kernels, local(): pl.pallas_call(functools.partial(kernel, share, na), out_shape=shapes, in...  81.3 us

profile of v4, /device:TPU:32, one launch (start us, length us, event | category | flops | bytes accessed | tf_op | source)
XLA Modules:
  0.0 83.5 jit_solution(11992170040811378110)
XLA Ops:
  0.6 81.3 %shard_map.49 = (f32[48,768]{1,0:T(8,128)}, f32[6,128]{1,0:T(8,128)}, f32[24,128]{1,0:T(8,128)}) custom-call(bf16[3072,768]{1,0:T(8,128)(2,1)} %pas_hbm.1, bf16[768,768]{1,0:T(8,128)(2,1)} %cen_hbm.1), custom_call_target="tpu_custom_call" | custom-call | flops 7247757312 | bytes 5898240 | tf_op jit(solution)/shard_map/pallas_call | solution.py:492
  81.9 1.6 %shard_map.50 = (f32[48,768]{1,0:T(8,128)}, f32[6,128]{1,0:T(8,128)}, f32[24,128]{1,0:T(8,128)}) custom-call(f32[48,768]{1,0:T(8,128)} %get-tuple-element.9.refs_0_, f32[6,128]{1,0:T(8,128)} %get-tuple-element.10.refs_1_, f32[24,128]{1,0:T(8,128)} %get-tuple-element.11.refs_2_), custom_call_target="tpu_custom_call" | custom-call | tf_op jit(solution)/shard_map/pallas_call | solution.py:539

commit v5 on v4

--- a/solution.py
+++ b/solution.py
@@ -253,7 +253,7 @@
 
         tops = lax.fori_loop(
             0, lists // 16, row_top,
-            tuple(jnp.full((8, 128), -jnp.inf, F32) for _ in range(2 * STEP)), unroll=8,
+            tuple(jnp.full((8, 128), -jnp.inf, F32) for _ in range(2 * STEP)), unroll=16,
         )
         tops = [jnp.max(jnp.maximum(tops[c], tops[c + STEP]), axis=0, keepdims=True) for c in range(STEP)]
         wide = [jnp.broadcast_to(top, (8, 128)) for top in tops]
@@ -270,7 +270,7 @@
             return tuple(out)
 
         sums = lax.fori_loop(
-            0, lists // 16, row_exp, tuple(jnp.zeros((8, 128), F32) for _ in range(2 * STEP)), unroll=8
+            0, lists // 16, row_exp, tuple(jnp.zeros((8, 128), F32) for _ in range(2 * STEP)), unroll=16
         )
         result = []
         for c, top in enumerate(tops):
@@ -303,7 +303,7 @@
             out[base, :] = total if start is None else total + start[base, :]
             return carry
 
-        lax.fori_loop(0, count // 8, body, 0, unroll=8)
+        lax.fori_loop(0, count // 8, body, 0, unroll=16)
 
     def row_sweep(b, h):
         cols = columns(b)
@@ -318,7 +318,7 @@
             return tuple(out)
 
         sums = lax.fori_loop(
-            0, lists // (16 * PARTS), body, tuple(jnp.zeros((8, 128), F32) for _ in range(2 * STEP)), unroll=8
+            0, lists // (16 * PARTS), body, tuple(jnp.zeros((8, 128), F32) for _ in range(2 * STEP)), unroll=16
         )
         return [sums[c] + sums[c + STEP] for c in range(STEP)], cols
 
@@ -529,7 +529,7 @@
             dma((3,)), dma((groups, 4, 3)),
         ],
         compiler_params=pltpu.CompilerParams(
-            collective_id=0, has_side_effects=True, vmem_limit_bytes=56 << 20
+            collective_id=0, has_side_effects=True, vmem_limit_bytes=60 << 20
         ),
         cost_estimate=pl.CostEstimate(
             flops=4 * rows * depth * lists, bytes_accessed=2 * (rows + lists) * depth,

time: 83.6 us -> 83.2 us (level)
  no operation moved by 1% of the time
where the time goes in v5:
time: 83.2 us; the launch traced here: 82.9 us
  Pallas kernels  82.2 us (99%)
    pallas_call x1, Pallas kernels, local(): pl.pallas_call(functools.partial(kernel, share, na), out_shape=shapes, in...  80.6 us

profile of v5, /device:TPU:32, one launch (start us, length us, event | category | flops | bytes accessed | tf_op | source)
XLA Modules:
  0.0 82.9 jit_solution(7448134411947955153)
XLA Ops:
  0.6 80.6 %shard_map.49 = (f32[48,768]{1,0:T(8,128)}, f32[6,128]{1,0:T(8,128)}, f32[24,128]{1,0:T(8,128)}) custom-call(bf16[3072,768]{1,0:T(8,128)(2,1)} %pas_hbm.1, bf16[768,768]{1,0:T(8,128)(2,1)} %cen_hbm.1), custom_call_target="tpu_custom_call" | custom-call | flops 7247757312 | bytes 5898240 | tf_op jit(solution)/shard_map/pallas_call | solution.py:492
  81.3 1.6 %shard_map.50 = (f32[48,768]{1,0:T(8,128)}, f32[6,128]{1,0:T(8,128)}, f32[24,128]{1,0:T(8,128)}) custom-call(f32[48,768]{1,0:T(8,128)} %get-tuple-element.9.refs_0_, f32[6,128]{1,0:T(8,128)} %get-tuple-element.10.refs_1_, f32[24,128]{1,0:T(8,128)} %get-tuple-element.11.refs_2_), custom_call_target="tpu_custom_call" | custom-call | tf_op jit(solution)/shard_map/pallas_call | solution.py:539
